TPU v7x, 32 devices: a whole 2x2x4 slice. The times are simulated.
32 devices in a mesh: chan: 8 (over z, y), tm: 4 (over x, core).
Axes of the slice: x: 2, y: 2, z: 4, core: 2. Of those that a mesh axis runs over, the one named last changes fastest.
Arguments:
- voltages: bfloat16 [32, 128, 2, 1024], P('chan', 'tm'), may hold values from -6 to 6
- filter_taps: float32 [12, 1024], replicated, may hold values from -1.75 to 1.75
- flagged: int32 [256], replicated, may hold values from 0 to 1023, as said below
- owners: int32 [1024], replicated, may hold values from 0 to 31, as said below
Outputs:
- visibilities: float32 [1024, 2, 32, 32], P(('chan', 'tm'))
Inputs may be any that keep to these rules, and one draw needn't show every extreme that they name: `flagged`: distinct channel numbers. `owners`: each device owns exactly 32 of the 1024 channels, flagged or not; device d is the one with chan index d // 4 and tm index d % 4.
All inputs are finite; a program needn't handle non-finite values.
Results may differ from a plain program's by a relative error of at most 0.0059.
Values may be sent and summed in bfloat16 or wider, within the bound.
A program may use at most 64 MiB of HBM per device.

v0:
```python
import math

import jax
import jax.numpy as jnp
import numpy as np
from jax import lax
from jax.sharding import PartitionSpec as P


def dft_table(channels):
    positions = np.arange(channels, dtype=np.int32)
    phases = positions[:, None] * positions[None, :] % channels
    angles = phases.astype(np.float32) * np.float32(2.0 * math.pi / channels)
    factor = np.float32(1.0 / math.sqrt(channels))
    table = np.concatenate([np.cos(angles) * factor, np.sin(angles) * factor], axis=1)
    return jnp.asarray(table.astype(jnp.bfloat16))


def slot_matrix(flagged, owners, channels, capacity):
    ids = jnp.arange(channels, dtype=jnp.int32)
    alive = jnp.logical_not(jnp.any(flagged[:, None] == ids[None, :], axis=0))
    earlier = (owners[None, :] == owners[:, None]) & alive[None, :] & (ids[None, :] < ids[:, None])
    rank = jnp.sum(earlier.astype(jnp.int32), axis=1)
    slot_of = jnp.where(alive, owners * capacity + rank, -1)
    return (slot_of[None, :] == ids[:, None]).astype(jnp.bfloat16)


def local(voltages, filter_taps, flagged, owners):
    inp_dev, spec_dev, _, channels = voltages.shape
    taps = filter_taps.shape[0]
    devices = lax.axis_size("chan") * lax.axis_size("tm")
    capacity = channels // devices
    picks = slot_matrix(flagged, owners, channels, capacity)
    mine = lax.all_to_all(voltages, "tm", split_axis=0, concat_axis=1, tiled=True)
    stations, spectra_all = mine.shape[:2]
    samples = mine.transpose(0, 2, 1, 3).astype(jnp.float32)
    padded = jnp.pad(samples, ((0, 0), (0, 0), (taps - 1, 0), (0, 0)))
    running = jnp.zeros(samples.shape, jnp.float32)
    for tap in range(taps):
        start = taps - 1 - tap
        running = running + filter_taps[tap] * padded[:, :, start : start + spectra_all]
    filtered = running.astype(jnp.bfloat16)
    turned = jnp.stack([filtered[:, 1], -filtered[:, 0]], axis=1)
    rows = stations * 2 * spectra_all
    both = jnp.concatenate([filtered, turned], axis=-1).reshape(rows, 2 * channels)
    spectra = lax.dot_general(
        dft_table(channels), both, (((1,), (1,)), ((), ())), preferred_element_type=jnp.float32
    ).astype(jnp.bfloat16)
    chosen = jnp.dot(picks, spectra, preferred_element_type=jnp.float32).astype(jnp.bfloat16)
    sending = chosen.reshape(devices, capacity, rows)
    received = lax.all_to_all(sending, ("chan", "tm"), split_axis=0, concat_axis=0, tiled=True)
    parts = received.reshape(devices, capacity, stations, 2 * spectra_all).transpose(1, 0, 2, 3)
    first = parts.reshape(capacity, devices * stations, 2 * spectra_all)
    second = jnp.concatenate([first[..., spectra_all:], -first[..., :spectra_all]], axis=-1)
    stacked = jnp.stack([first, second], axis=1)
    total = jnp.einsum("cpit,cjt->cpij", stacked, first, preferred_element_type=jnp.float32)
    return total / spectra_all


def solution(mesh):
    return jax.shard_map(
        local,
        mesh=mesh,
        in_specs=(P("chan", "tm", None, None), P(), P(), P()),
        out_specs=P(("chan", "tm"), None, None, None),
        check_vma=False,
    )
```

profile of v0, /device:TPU:0, one launch (start us, length us, event | category | flops | bytes accessed | tf_op | source)
XLA Modules:
  0.0 41.9 jit_solution(1879193986597163640)
XLA Ops:
  0.0 4.2 %all-to-all-start = ((bf16[4,32,2,1024]{3,2,1,0:T(2,128)(2,1)}), bf16[4,32,2,1024]{3,2,1,0:T(2,128)(2,1)S(1)}, u32[]{:S(2)}, u32[]{:S(2)}) async-start(bf16[4,32,2,1024]{3,2,1,0:T(2,128)(2,1)} %param.5), calls=%async_computation | async-start | bytes 1048576 | tf_op jit(solution)/shard_map/all_to_all | solution.py:34
  4.2 0.9 %fusion.27 = pred[1024]{0:T(1024)(128)(4,1)S(1)} fusion(s32[256]{0:T(256)} %param.7), kind=kLoop, calls=%fused_computation.46 | loop fusion | flops 523264 | bytes 2048 | tf_op jit(solution)/shard_map/reduce_or | solution.py:21
  5.1 1.4 %convert_reduce_fusion = s32[1024]{0:T(1024)S(1)} fusion(s32[1024]{0:T(1024)} %param.8, pred[1024]{0:T(1024)(128)(4,1)S(1)} %not.7), kind=kLoop, calls=%fused_computation.1 | loop fusion | flops 6290432 | bytes 9216 | tf_op jit(solution)/shard_map/reduce_sum | solution.py:23
  6.5 0.7 %add_select_fusion = s32[1024]{0:T(1024)S(1)} fusion(pred[1024]{0:T(1024)(128)(4,1)S(1)} %fusion.27, s32[1024]{0:T(1024)S(1)} %convert_reduce_fusion, s32[1024]{0:T(1024)} %param.8), kind=kLoop, calls=%fused_computation.55 | loop fusion | flops 3072 | bytes 13312 | tf_op jit(solution)/shard_map/jit(_where)/select_n | solution.py:24
  7.2 1.3 %fusion.33 = (f32[1,1024]{1,0:T(1,128)S(1)}, f32[1,1024]{1,0:T(1,128)S(1)}, f32[1,1024]{1,0:T(1,128)S(1)}, f32[1,1024]{1,0:T(1,128)S(1)}, f32[1,1024]{1,0:T(1,12...) fusion(f32[12,1024]{1,0:T(8,128)} %param.6), kind=kLoop, calls=%fused_computation.58 | loop fusion | bytes 98304 | tf_op jit(solution)/shard_map/slice | solution.py:41
  8.5 4.6 %all-to-all-done = bf16[4,32,2,1024]{3,2,1,0:T(2,128)(2,1)S(1)} async-done(((bf16[4,32,2,1024]{3,2,1,0:T(2,128)(2,1)}), bf16[4,32,2,1024]{3,2,1,0:T(2,128)(2,1)S(1)}, u32[]{:S(2)}, u32[]{:S(2)}) %all-to-all-start) | async-done | bytes 524320 | tf_op jit(solution)/shard_map/all_to_all | solution.py:34
  13.1 0.1 copy.14
  13.2 1.3 %fusion.28 = bf16[1,2,128,1024]{3,2,1,0:T(8,128)(2,1)S(1)} fusion(f32[1,2,128,1024]{3,2,1,0:T(8,128)S(1)} %bitcast.37, f32[1024]{0:T(1024)S(1)} %bitcast.52, f32[1024]{0:T(1024)S(1)} %bitcast.53, f32[1024]{0:T(1024)S(1)} %bitcast.43, f32[1024]{0:T(1024)S(1)} %bitcast.44, f32[1024]{0:T(1024)S(1)} %bitcast.45, f32[1024]{0:T(1024)S(1)} %bitcast.46, ...), kind=kLoop, calls=%fused_computation.47 | loop fusion | flops 6291456 | bytes 1622016 | tf_op jit(solution)/shard_map/convert_element_type | solution.py:42
  14.6 0.1 maximum_maximum_fusion
  14.6 4.3 %fusion.3 = bf16[1024,256]{1,0:T(8,128)(2,1)S(1)} fusion(s32[1024]{0:T(1024)S(1)} %add_select_fusion, bf16[256,2048]{1,0:T(8,128)(2,1)S(1)} %bitcast.40, bf16[1024,2048]{1,0:T(8,128)(2,1)} %constant.15.clone), kind=kOutput, calls=%fused_computation.7 | convolution fusion | flops 1612185600 | bytes 5771264 | tf_op jit(solution)/shard_map/dot_general | solution.py:49
  19.0 21.0 %all_to_all.14 = bf16[32,32,256]{2,1,0:T(8,128)(2,1)S(1)} all-to-all(bf16[32,32,256]{2,1,0:T(8,128)(2,1)S(1)} %bitcast.41), channel_id=1, replica_groups=mesh['chan'=8,'tm'=4] {'chan','tm'}, dimensions={0} | all-to-all | bytes 1048576 | tf_op jit(solution)/shard_map/all_to_all | solution.py:51
  39.9 0.3 copy.26
  40.2 0.1 fusion.31
  40.3 0.1 maximum_bitcast_fusion
  40.4 1.5 %convolution_multiply_fusion = f32[32,2,32,32]{3,2,1,0:T(8,128)} fusion(bf16[32,32,256]{2,1,0:T(8,128)(2,1)S(1)} %all_to_all.14, bf16[32,1,32,256]{3,2,0,1:T(8,128)(2,1)S(1)} %maximum_bitcast_fusion, bf16[32,1,32,256]{3,2,0,1:T(8,128)(2,1)S(1)} %bitcast.39), kind=kOutput, calls=%fused_computation.6 | convolution fusion | flops 34144256 | bytes 1835008 | tf_op jit(solution)/shard_map/cpit,cjt->cpij/dot_general | solution.py:56
  (2 shorter events, 0.0 us)
Async XLA Ops:
  0.0 13.1 %all-to-all-start = ((bf16[4,32,2,1024]{3,2,1,0:T(2,128)(2,1)}), bf16[4,32,2,1024]{3,2,1,0:T(2,128)(2,1)S(1)}, u32[]{:S(2)}, u32[]{:S(2)}) async-start(bf16[4,32,2,1024]{3,2,1,0:T(2,128)(2,1)} %param.5), calls=%async_computation | async-start | bytes 1048576 | tf_op jit(solution)/shard_map/all_to_all | solution.py:34
where the time goes:
time: 42.3 us; the launch traced here: 41.9 us
  blocking collectives  21 us (50%)
  matrix products  5.83 us (14%)
  waiting for transfers between devices  4.58 us (11%)
  other arithmetic  4.53 us (11%)
  starting transfers between devices  4.21 us (10%)
  local copies, waits for them, and re-layouts  1.71 us (4%)
    all_to_all x1, blocking collectives, local(): lax.all_to_all(sending, ('chan', 'tm'), split_axis=0, concat_axis=0, tile...  21 us
    all_to_all x1, waiting for transfers between devices, local(): lax.all_to_all(voltages, 'tm', split_axis=0, concat_axis=1, tiled=True)  4.58 us
    dot_general x1, matrix products, local(): jnp.dot(picks, spectra, preferred_element_type=jnp.float32)  4.33 us
    all_to_all x1, starting transfers between devices, local(): lax.all_to_all(voltages, 'tm', split_axis=0, concat_axis=1, tiled=True)  4.21 us
    dot_general x1, matrix products, local(): jnp.einsum('cpit,cjt->cpij', stacked, first, preferred_element_type=jnp.f...  1.5 us
    reduce_sum x1, other arithmetic, slot_matrix(): rank = jnp.sum(earlier.astype(jnp.int32), axis=1)  1.37 us
    convert_element_type x1, other arithmetic, local(): filtered = running.astype(jnp.bfloat16)  1.31 us
    slice x1, local copies, waits for them, and re-layouts, local(): filter_taps[tap] * padded[:, :, start:start + spectra_all]  1.28 us
  transfers between devices with their start and end apart: 1, of which 1 were waited for; matrix products, arithmetic and copies ran while one was open for 10% of the time, Pallas kernels for 0%

commit v1 on v0

--- a/solution.py
+++ b/solution.py
@@ -1,9 +1,12 @@
+import functools
 import math
 
 import jax
 import jax.numpy as jnp
 import numpy as np
 from jax import lax
+from jax.experimental import pallas as pl
+from jax.experimental.pallas import tpu as pltpu
 from jax.sharding import PartitionSpec as P
 
 
@@ -25,6 +28,101 @@
     return (slot_of[None, :] == ids[:, None]).astype(jnp.bfloat16)
 
 
+GROUP_ROWS = 256
+MESH = pl.DeviceIdType.MESH
+
+
+def turn_kernel(chans, times, both_ref, table, picks_ref, got_ref, spectra, sending, send_sem, recv_sem):
+    devices = chans * times
+    capacity = sending.shape[1]
+    channels = table.shape[0]
+    per_group = GROUP_ROWS // capacity
+    groups = devices // per_group
+    me = lax.axis_index("chan") * times + lax.axis_index("tm")
+
+    barrier = pltpu.get_barrier_semaphore()
+
+    def greet(step, carry):
+        other = lax.rem(me + step, devices)
+        pl.semaphore_signal(barrier, inc=1, device_id=(other // times, lax.rem(other, times)), device_id_type=MESH)
+        return carry
+
+    lax.fori_loop(1, devices, greet, 0)
+
+    def block_copy(slot_block, source, other):
+        return pltpu.make_async_remote_copy(
+            src_ref=sending.at[slot_block],
+            dst_ref=got_ref.at[source],
+            send_sem=send_sem.at[slot_block],
+            recv_sem=recv_sem.at[source],
+            device_id=(other // times, lax.rem(other, times)),
+            device_id_type=MESH,
+        )
+
+    def transform(step, carry):
+        rows = pl.ds(pl.multiple_of(step * GROUP_ROWS, GROUP_ROWS), GROUP_ROWS)
+        spectra[rows, :] = lax.dot_general(
+            table[rows, :], both_ref[...], (((1,), (1,)), ((), ())), preferred_element_type=jnp.float32
+        ).astype(jnp.bfloat16)
+        return carry
+
+    lax.fori_loop(0, channels // GROUP_ROWS, transform, 0)
+    pl.semaphore_wait(barrier, devices - 1)
+
+    def send_group(step, carry):
+        group = lax.rem(me // per_group + groups // 2 + step, groups)
+        rows = pl.ds(pl.multiple_of(group * GROUP_ROWS, GROUP_ROWS), GROUP_ROWS)
+        chosen = jnp.dot(picks_ref[rows, :], spectra[...], preferred_element_type=jnp.float32)
+        sending[pl.ds(group * per_group, per_group)] = chosen.astype(jnp.bfloat16).reshape(
+            per_group, capacity, chosen.shape[1]
+        )
+
+        def send(position, inner):
+            other = group * per_group + lax.rem(me + position, per_group)
+
+            @pl.when(other != me)
+            def _():
+                block_copy(other, me, other).start()
+
+            return inner
+
+        lax.fori_loop(0, per_group, send, 0)
+        return carry
+
+    lax.fori_loop(0, groups, send_group, 0)
+    got_ref[me] = sending[me]
+
+    def finish(step, carry):
+        other = lax.rem(me + step, devices)
+        copy = block_copy(other, other, other)
+        copy.wait_send()
+        copy.wait_recv()
+        return carry
+
+    lax.fori_loop(1, devices, finish, 0)
+
+
+def turn(both, table, picks, chans, times, capacity):
+    devices = chans * times
+    rows = both.shape[0]
+    channels = table.shape[0]
+    return pl.pallas_call(
+        functools.partial(turn_kernel, chans, times),
+        out_shape=jax.ShapeDtypeStruct((devices, capacity, rows), jnp.bfloat16),
+        in_specs=[pl.BlockSpec(memory_space=pltpu.VMEM)] * 3,
+        out_specs=pl.BlockSpec(memory_space=pltpu.VMEM),
+        scratch_shapes=[
+            pltpu.VMEM((channels, rows), jnp.bfloat16),
+            pltpu.VMEM((devices, capacity, rows), jnp.bfloat16),
+            pltpu.SemaphoreType.DMA((devices,)),
+            pltpu.SemaphoreType.DMA((devices,)),
+        ],
+        compiler_params=pltpu.CompilerParams(
+            collective_id=0, has_side_effects=True, vmem_limit_bytes=32 * 1024 * 1024
+        ),
+    )(both, table, picks)
+
+
 def local(voltages, filter_taps, flagged, owners):
     inp_dev, spec_dev, _, channels = voltages.shape
     taps = filter_taps.shape[0]
@@ -43,12 +141,16 @@
     turned = jnp.stack([filtered[:, 1], -filtered[:, 0]], axis=1)
     rows = stations * 2 * spectra_all
     both = jnp.concatenate([filtered, turned], axis=-1).reshape(rows, 2 * channels)
-    spectra = lax.dot_general(
-        dft_table(channels), both, (((1,), (1,)), ((), ())), preferred_element_type=jnp.float32
-    ).astype(jnp.bfloat16)
-    chosen = jnp.dot(picks, spectra, preferred_element_type=jnp.float32).astype(jnp.bfloat16)
-    sending = chosen.reshape(devices, capacity, rows)
-    received = lax.all_to_all(sending, ("chan", "tm"), split_axis=0, concat_axis=0, tiled=True)
+    table = dft_table(channels)
+    if capacity % 16 == 0 and GROUP_ROWS % capacity == 0 and channels % GROUP_ROWS == 0:
+        received = turn(both, table, picks, lax.axis_size("chan"), lax.axis_size("tm"), capacity)
+    else:
+        spectra = lax.dot_general(
+            table, both, (((1,), (1,)), ((), ())), preferred_element_type=jnp.float32
+        ).astype(jnp.bfloat16)
+        chosen = jnp.dot(picks, spectra, preferred_element_type=jnp.float32).astype(jnp.bfloat16)
+        sending = chosen.reshape(devices, capacity, rows)
+        received = lax.all_to_all(sending, ("chan", "tm"), split_axis=0, concat_axis=0, tiled=True)
     parts = received.reshape(devices, capacity, stations, 2 * spectra_all).transpose(1, 0, 2, 3)
     first = parts.reshape(capacity, devices * stations, 2 * spectra_all)
     second = jnp.concatenate([first[..., spectra_all:], -first[..., :spectra_all]], axis=-1)

time: 42.3 us -> 35.8 us (0.85)
  the two profiles are of different devices: /device:TPU:0 before, /device:TPU:9 now
where the time goes in v1:
time: 35.8 us; the launch traced here: 35.4 us
  Pallas kernels  18.8 us (53%)
  other arithmetic  5.62 us (16%)
  starting transfers between devices  4.11 us (11%)
  waiting for transfers between devices  2.82 us (8%)
  matrix products  2.05 us (6%)
  local copies, waits for them, and re-layouts  1.91 us (5%)
    pallas_call x1, Pallas kernels, turn(): pl.pallas_call(functools.partial(turn_kernel, chans, times), out_shape=ja...  18.8 us
    all_to_all x1, starting transfers between devices, local(): lax.all_to_all(voltages, 'tm', split_axis=0, concat_axis=1, tiled=True)  4.11 us
    all_to_all x1, waiting for transfers between devices, local(): lax.all_to_all(voltages, 'tm', split_axis=0, concat_axis=1, tiled=True)  2.82 us
    dot_general x1, matrix products, local(): jnp.einsum('cpit,cjt->cpij', stacked, first, preferred_element_type=jnp.f...  2.05 us
    reduce_sum x1, other arithmetic, slot_matrix(): rank = jnp.sum(earlier.astype(jnp.int32), axis=1)  1.37 us
    convert_element_type x1, other arithmetic, local(): filtered = running.astype(jnp.bfloat16)  1.31 us
    slice x1, local copies, waits for them, and re-layouts, local(): filter_taps[tap] * padded[:, :, start:start + spectra_all]  1.29 us
    reduce_or x1, other arithmetic, slot_matrix(): alive = jnp.logical_not(jnp.any(flagged[:, None] == ids[None, :], axis=0))  0.89 us
  transfers between devices with their start and end apart: 1, of which 1 were waited for; matrix products, arithmetic and copies ran while one was open for 15% of the time, Pallas kernels for 0%

profile of v1, /device:TPU:9, one launch (start us, length us, event | category | flops | bytes accessed | tf_op | source)
XLA Modules:
  0.0 35.4 jit_solution(3682223380459817589)
XLA Ops:
  0.0 4.1 %all-to-all-start = ((bf16[4,32,2,1024]{3,2,1,0:T(2,128)(2,1)}), bf16[4,32,2,1024]{3,2,1,0:T(2,128)(2,1)S(1)}, u32[]{:S(2)}, u32[]{:S(2)}) async-start(bf16[4,32,2,1024]{3,2,1,0:T(2,128)(2,1)} %param.5), calls=%async_computation | async-start | bytes 1048576 | tf_op jit(solution)/shard_map/all_to_all | solution.py:132
  4.1 0.9 %fusion.25 = pred[1024]{0:T(1024)(128)(4,1)S(1)} fusion(s32[256]{0:T(256)} %param.7), kind=kLoop, calls=%fused_computation.44 | loop fusion | flops 523264 | bytes 2048 | tf_op jit(solution)/shard_map/reduce_or | solution.py:24
  5.0 1.3 %fusion.30 = (f32[1,1024]{1,0:T(1,128)S(1)}, f32[1,1024]{1,0:T(1,128)S(1)}, f32[1,1024]{1,0:T(1,128)S(1)}, f32[1,1024]{1,0:T(1,128)S(1)}, f32[1,1024]{1,0:T(1,12...) fusion(f32[12,1024]{1,0:T(8,128)} %param.6), kind=kLoop, calls=%fused_computation.54 | loop fusion | bytes 98304 | tf_op jit(solution)/shard_map/slice | solution.py:139
  6.3 1.4 %convert_reduce_fusion = s32[1024]{0:T(1024)S(1)} fusion(s32[1024]{0:T(1024)} %param.8, pred[1024]{0:T(1024)(128)(4,1)S(1)} %not.7), kind=kLoop, calls=%fused_computation.1 | loop fusion | flops 6290432 | bytes 9216 | tf_op jit(solution)/shard_map/reduce_sum | solution.py:26
  7.7 0.7 %add_select_fusion = s32[1024]{0:T(1024)S(1)} fusion(pred[1024]{0:T(1024)(128)(4,1)S(1)} %fusion.25, s32[1024]{0:T(1024)S(1)} %convert_reduce_fusion, s32[1024]{0:T(1024)} %param.8), kind=kLoop, calls=%fused_computation.51 | loop fusion | flops 3072 | bytes 13312 | tf_op jit(solution)/shard_map/jit(_where)/select_n | solution.py:27
  8.4 0.9 %fusion.1.picks_ref = bf16[1024,1024]{1,0:T(8,128)(2,1)S(1)} fusion(s32[1024]{0:T(1024)S(1)} %add_select_fusion), kind=kLoop, calls=%fused_computation.4 | loop fusion | flops 2097152 | bytes 2101248 | tf_op jit(solution)/shard_map/convert_element_type | solution.py:28
  9.3 2.8 %all-to-all-done = bf16[4,32,2,1024]{3,2,1,0:T(2,128)(2,1)S(1)} async-done(((bf16[4,32,2,1024]{3,2,1,0:T(2,128)(2,1)}), bf16[4,32,2,1024]{3,2,1,0:T(2,128)(2,1)S(1)}, u32[]{:S(2)}, u32[]{:S(2)}) %all-to-all-start) | async-done | bytes 524320 | tf_op jit(solution)/shard_map/all_to_all | solution.py:132
  12.1 0.0 copy-start
  12.1 0.1 bitcast_convert_fusion
  12.2 0.3 copy.20
  12.6 1.3 %fusion.26 = bf16[1,2,128,1024]{3,2,1,0:T(8,128)(2,1)S(1)} fusion(f32[1,2,128,1024]{3,2,1,0:T(8,128)S(1)} %bitcast.37, f32[1024]{0:T(1024)S(1)} %bitcast.50, f32[1024]{0:T(1024)S(1)} %bitcast.51, f32[1024]{0:T(1024)S(1)} %bitcast.41, f32[1024]{0:T(1024)S(1)} %bitcast.42, f32[1024]{0:T(1024)S(1)} %bitcast.43, f32[1024]{0:T(1024)S(1)} %bitcast.44, ...), kind=kLoop, calls=%fused_computation.45 | loop fusion | flops 6291456 | bytes 1622016 | tf_op jit(solution)/shard_map/convert_element_type | solution.py:140
  13.9 0.1 maximum_maximum_fusion
  14.0 0.3 copy-done
  14.3 18.8 %shard_map.55 = bf16[32,32,256]{2,1,0:T(8,128)(2,1)S(1)} custom-call(bf16[256,2048]{1,0:T(8,128)(2,1)S(1)} %bitcast.36, bf16[1024,2048]{1,0:T(8,128)(2,1)S(1)} %copy-done, bf16[1024,1024]{1,0:T(8,128)(2,1)S(1)} %fusion.1.picks_ref), custom_call_target="tpu_custom_call" | custom-call | tf_op jit(solution)/shard_map/pallas_call | solution.py:109
  33.1 0.1 fusion.28
  33.1 0.1 maximum_bitcast_fusion
  33.2 0.1 pad_maximum_fusion
  33.3 2.1 %convolution_multiply_fusion = f32[32,2,32,32]{3,2,1,0:T(8,128)} fusion(bf16[32,2,32,256]{3,0,2,1:T(8,128)(2,1)S(1)} %pad_maximum_fusion, bf16[32,32,256,1]{2,0,1,3:T(8,128)(2,1)S(1)} %bitcast.35), kind=kOutput, calls=%fused_computation.5 | convolution fusion | flops 33619968 | bytes 1835008 | tf_op jit(solution)/shard_map/cpit,cjt->cpij/dot_general | solution.py:158
  (2 shorter events, 0.0 us)
Async XLA Ops:
  0.0 12.1 %all-to-all-start = ((bf16[4,32,2,1024]{3,2,1,0:T(2,128)(2,1)}), bf16[4,32,2,1024]{3,2,1,0:T(2,128)(2,1)S(1)}, u32[]{:S(2)}, u32[]{:S(2)}) async-start(bf16[4,32,2,1024]{3,2,1,0:T(2,128)(2,1)} %param.5), calls=%async_computation | async-start | bytes 1048576 | tf_op jit(solution)/shard_map/all_to_all | solution.py:132
  12.1 2.2 %copy-start = (bf16[1024,2048]{1,0:T(8,128)(2,1)S(1)}, bf16[1024,2048]{1,0:T(8,128)(2,1)}, u32[]{:S(2)}) copy-start(bf16[1024,2048]{1,0:T(8,128)(2,1)} %constant.15.clone.table) | copy-start | bytes 12582916

commit v2 on v1

--- a/solution.py
+++ b/solution.py
@@ -32,10 +32,12 @@
 MESH = pl.DeviceIdType.MESH
 
 
-def turn_kernel(chans, times, both_ref, table, picks_ref, got_ref, spectra, sending, send_sem, recv_sem):
+def turn_kernel(chans, times, halo_ref, fresh_ref, taps_ref, table, picks_ref, order_ref, out_ref, wide, both_ref, spectra, got_ref, sending, send_sem, recv_sem):
     devices = chans * times
-    capacity = sending.shape[1]
+    capacity, rows_all = sending.shape[1:]
     channels = table.shape[0]
+    stations = out_ref.shape[1]
+    halo, spec_dev = halo_ref.shape[0], fresh_ref.shape[0]
     per_group = GROUP_ROWS // capacity
     groups = devices // per_group
     me = lax.axis_index("chan") * times + lax.axis_index("tm")
@@ -49,10 +51,39 @@
 
     lax.fori_loop(1, devices, greet, 0)
 
+    def place(source):
+        return lax.rem(source, times) * chans + source // times
+
+    def widen(step, carry):
+        wide[halo + step] = fresh_ref[step].astype(jnp.float32)
+        return carry
+
+    for step in range(halo):
+        wide[step] = halo_ref[step].astype(jnp.float32)
+    lax.fori_loop(0, spec_dev, widen, 0)
+    series = fresh_ref.shape[1]
+    real_row = lax.broadcasted_iota(jnp.int32, (series, channels), 0) < series // 2
+
+    def filter_two(step, carry):
+        sums, turns = [], []
+        for half in range(2):
+            total = jnp.zeros((series, channels), jnp.float32)
+            for tap in range(halo + 1):
+                total = total + taps_ref[pl.ds(tap, 1), :] * wide[2 * step + half + halo - tap]
+            swapped = pltpu.roll(total, series // 2, 0)
+            sums.append(total)
+            turns.append(jnp.where(real_row, swapped, -swapped))
+        rows = pl.ds(pl.multiple_of(step * 2 * series, 2 * series), 2 * series)
+        both_ref[rows, :channels] = jnp.concatenate(sums, axis=0).astype(jnp.bfloat16)
+        both_ref[rows, channels:] = jnp.concatenate(turns, axis=0).astype(jnp.bfloat16)
+        return carry
+
+    lax.fori_loop(0, spec_dev // 2, filter_two, 0)
+
     def block_copy(slot_block, source, other):
         return pltpu.make_async_remote_copy(
             src_ref=sending.at[slot_block],
-            dst_ref=got_ref.at[source],
+            dst_ref=got_ref.at[place(source)],
             send_sem=send_sem.at[slot_block],
             recv_sem=recv_sem.at[source],
             device_id=(other // times, lax.rem(other, times)),
@@ -90,7 +121,7 @@
         return carry
 
     lax.fori_loop(0, groups, send_group, 0)
-    got_ref[me] = sending[me]
+    got_ref[place(me)] = sending[me]
 
     def finish(step, carry):
         other = lax.rem(me + step, devices)
@@ -101,18 +132,31 @@
 
     lax.fori_loop(1, devices, finish, 0)
 
-
-def turn(both, table, picks, chans, times, capacity):
+    for station in range(stations):
+        total = jnp.zeros((chans * capacity, rows_all), jnp.float32)
+        for block in range(times):
+            total = total + jnp.dot(
+                got_ref[block * chans : (block + 1) * chans].reshape(chans * capacity, rows_all),
+                order_ref[block * rows_all : (block + 1) * rows_all, station * rows_all : (station + 1) * rows_all],
+                preferred_element_type=jnp.float32,
+            )
+        out_ref[:, station] = total.astype(jnp.bfloat16).reshape(chans, capacity, rows_all)
+
+
+def turn(before, fresh, filter_taps, table, picks, order, chans, times, capacity):
     devices = chans * times
-    rows = both.shape[0]
-    channels = table.shape[0]
+    spec_dev, series, channels = fresh.shape
+    rows = spec_dev * series
     return pl.pallas_call(
         functools.partial(turn_kernel, chans, times),
-        out_shape=jax.ShapeDtypeStruct((devices, capacity, rows), jnp.bfloat16),
-        in_specs=[pl.BlockSpec(memory_space=pltpu.VMEM)] * 3,
+        out_shape=jax.ShapeDtypeStruct((chans, series // 2, capacity, rows), jnp.bfloat16),
+        in_specs=[pl.BlockSpec(memory_space=pltpu.VMEM)] * 6,
         out_specs=pl.BlockSpec(memory_space=pltpu.VMEM),
         scratch_shapes=[
+            pltpu.VMEM((before.shape[0] + spec_dev, series, channels), jnp.float32),
+            pltpu.VMEM((rows, 2 * channels), jnp.bfloat16),
             pltpu.VMEM((channels, rows), jnp.bfloat16),
+            pltpu.VMEM((devices, capacity, rows), jnp.bfloat16),
             pltpu.VMEM((devices, capacity, rows), jnp.bfloat16),
             pltpu.SemaphoreType.DMA((devices,)),
             pltpu.SemaphoreType.DMA((devices,)),
@@ -120,39 +164,53 @@
         compiler_params=pltpu.CompilerParams(
             collective_id=0, has_side_effects=True, vmem_limit_bytes=32 * 1024 * 1024
         ),
-    )(both, table, picks)
+    )(before, fresh, filter_taps, table, picks, order)
+
+
+def lane_order(stations, spec_dev, blocks):
+    shape = (blocks, spec_dev, 2, stations)
+    places = np.arange(math.prod(shape)).reshape(shape).transpose(3, 2, 0, 1).reshape(-1)
+    table = np.zeros((places.size, places.size), np.float32)
+    table[places, np.arange(places.size)] = 1.0
+    return jnp.asarray(table.astype(jnp.bfloat16))
 
 
 def local(voltages, filter_taps, flagged, owners):
-    inp_dev, spec_dev, _, channels = voltages.shape
-    taps = filter_taps.shape[0]
-    devices = lax.axis_size("chan") * lax.axis_size("tm")
+    stations, spec_dev, _, channels = voltages.shape
+    halo = filter_taps.shape[0] - 1
+    chans, times = lax.axis_size("chan"), lax.axis_size("tm")
+    devices = chans * times
     capacity = channels // devices
+    spectra_all = spec_dev * times
+    rows = 2 * stations * spec_dev
+    fresh = voltages.transpose(1, 2, 0, 3).reshape(spec_dev, 2 * stations, channels)
+    before = lax.ppermute(fresh[spec_dev - halo :], "tm", [(i, i + 1) for i in range(times - 1)])
     picks = slot_matrix(flagged, owners, channels, capacity)
-    mine = lax.all_to_all(voltages, "tm", split_axis=0, concat_axis=1, tiled=True)
-    stations, spectra_all = mine.shape[:2]
-    samples = mine.transpose(0, 2, 1, 3).astype(jnp.float32)
-    padded = jnp.pad(samples, ((0, 0), (0, 0), (taps - 1, 0), (0, 0)))
-    running = jnp.zeros(samples.shape, jnp.float32)
-    for tap in range(taps):
-        start = taps - 1 - tap
-        running = running + filter_taps[tap] * padded[:, :, start : start + spectra_all]
-    filtered = running.astype(jnp.bfloat16)
-    turned = jnp.stack([filtered[:, 1], -filtered[:, 0]], axis=1)
-    rows = stations * 2 * spectra_all
-    both = jnp.concatenate([filtered, turned], axis=-1).reshape(rows, 2 * channels)
     table = dft_table(channels)
+    order = lane_order(stations, spec_dev, times)
     if capacity % 16 == 0 and GROUP_ROWS % capacity == 0 and channels % GROUP_ROWS == 0:
-        received = turn(both, table, picks, lax.axis_size("chan"), lax.axis_size("tm"), capacity)
+        first = turn(before, fresh, filter_taps, table, picks, order, chans, times, capacity)
+        first = first.reshape(chans * stations, capacity, 2 * spectra_all).transpose(1, 0, 2)
     else:
+        joined = jnp.concatenate([before, fresh]).astype(jnp.float32)
+        running = jnp.zeros(fresh.shape, jnp.float32)
+        for tap in range(halo + 1):
+            start = halo - tap
+            running = running + filter_taps[tap] * joined[start : start + spec_dev]
+        turned = jnp.concatenate([running[:, stations:], -running[:, :stations]], axis=1)
+        both = jnp.concatenate([running, turned], axis=-1).astype(jnp.bfloat16).reshape(rows, 2 * channels)
         spectra = lax.dot_general(
             table, both, (((1,), (1,)), ((), ())), preferred_element_type=jnp.float32
         ).astype(jnp.bfloat16)
         chosen = jnp.dot(picks, spectra, preferred_element_type=jnp.float32).astype(jnp.bfloat16)
         sending = chosen.reshape(devices, capacity, rows)
         received = lax.all_to_all(sending, ("chan", "tm"), split_axis=0, concat_axis=0, tiled=True)
-    parts = received.reshape(devices, capacity, stations, 2 * spectra_all).transpose(1, 0, 2, 3)
-    first = parts.reshape(capacity, devices * stations, 2 * spectra_all)
+        parts = received.reshape(chans, times, capacity, rows).transpose(0, 2, 1, 3)
+        ordered = jnp.dot(
+            parts.reshape(chans * capacity, times * rows), order, preferred_element_type=jnp.float32
+        ).astype(jnp.bfloat16)
+        first = ordered.reshape(chans, capacity, stations, 2 * spectra_all).transpose(1, 0, 2, 3)
+        first = first.reshape(capacity, chans * stations, 2 * spectra_all)
     second = jnp.concatenate([first[..., spectra_all:], -first[..., :spectra_all]], axis=-1)
     stacked = jnp.stack([first, second], axis=1)
     total = jnp.einsum("cpit,cjt->cpij", stacked, first, preferred_element_type=jnp.float32)

time: 35.8 us -> 34.7 us (0.969)
  the two profiles are of different devices: /device:TPU:9 before, /device:TPU:0 now
where the time goes in v2:
time: 34.7 us; the launch traced here: 34.3 us
  Pallas kernels  20.3 us (59%)
  local copies, waits for them, and re-layouts  6.05 us (17%)
  other arithmetic  3.99 us (11%)
  starting transfers between devices  2.35 us (7%)
  matrix products  1.53 us (4%)
    pallas_call x1, Pallas kernels, turn(): pl.pallas_call(functools.partial(turn_kernel, chans, times), out_shape=ja...  20.3 us
    ppermute x1, starting transfers between devices, local(): lax.ppermute(fresh[spec_dev - halo:], 'tm', [(i, i + 1) for i in range(ti...  2.35 us
    unnamed x6, local copies, waits for them, and re-layouts  2.19 us
    slice x3, local copies, waits for them, and re-layouts, local(): fresh[spec_dev - halo:]  1.99 us
    dot_general x1, matrix products, local(): jnp.einsum('cpit,cjt->cpij', stacked, first, preferred_element_type=jnp.f...  1.53 us
    transpose x1, local copies, waits for them, and re-layouts, local(): voltages.transpose(1, 2, 0, 3).reshape(spec_dev, 2 * stations, channels)  1.45 us
    reduce_sum x1, other arithmetic, slot_matrix(): rank = jnp.sum(earlier.astype(jnp.int32), axis=1)  1.37 us
    reduce_or x1, other arithmetic, slot_matrix(): alive = jnp.logical_not(jnp.any(flagged[:, None] == ids[None, :], axis=0))  0.89 us
  transfers between devices with their start and end apart: 1, of which 0 were waited for; matrix products, arithmetic and copies ran while one was open for 16% of the time, Pallas kernels for 0%

profile of v2, /device:TPU:0, one launch (start us, length us, event | category | flops | bytes accessed | tf_op | source)
XLA Modules:
  0.0 34.3 jit_solution(10988448280814424037)
XLA Ops:
  0.0 0.0 copy-start.1
  0.0 0.0 copy-start.2
  0.0 1.2 %slice.16 = bf16[11,2,4,1024]{3,1,0,2:T(2,128)(2,1)S(1)} slice(bf16[32,2,4,1024]{3,1,0,2:T(2,128)(2,1)} %bitcast.22), slice={[21:32], [0:2], [0:4], [0:1024]} | slice | bytes 360448 | tf_op jit(solution)/shard_map/slice | solution.py:187
  1.2 0.1 copy.11
  1.3 0.7 %slice.13 = bf16[11,8,1024]{2,1,0:T(8,128)(2,1)} reshape(bf16[11,2,4,1024]{3,2,1,0:T(4,128)(2,1)S(1)} %copy.11) | data formatting | bytes 360448 | tf_op jit(solution)/shard_map/slice | solution.py:187
  2.0 2.4 %collective-permute-start = (bf16[11,8,1024]{2,1,0:T(8,128)(2,1)}, bf16[11,8,1024]{2,1,0:T(8,128)(2,1)S(1)}, u32[]{:S(2)}, u32[]{:S(2)}) collective-permute-start(bf16[11,8,1024]{2,1,0:T(8,128)(2,1)} %slice.13), channel_id=1, source_target_pairs={{0,1},{1,2},{2,3},{4,5},{5,6},{6,7},{8,9},{9,10},{10,11},{12,13},{... | collective-permute-start | bytes 540680 | tf_op jit(solution)/shard_map/ppermute | solution.py:187
  4.4 1.5 %copy.12 = bf16[32,2,4,1024]{3,2,1,0:T(4,128)(2,1)S(1)} copy(bf16[32,2,4,1024]{3,1,0,2:T(2,128)(2,1)} %bitcast.23) | data formatting | bytes 1048576 | tf_op jit(solution)/shard_map/transpose | solution.py:186
  5.8 0.9 %fusion.5 = pred[1024]{0:T(1024)(128)(4,1)S(1)} fusion(s32[256]{0:T(256)} %param.8), kind=kLoop, calls=%fused_computation.10 | loop fusion | flops 523264 | bytes 2048 | tf_op jit(solution)/shard_map/reduce_or | solution.py:24
  6.7 1.4 %convert_reduce_fusion = s32[1024]{0:T(1024)S(1)} fusion(s32[1024]{0:T(1024)} %param.9, pred[1024]{0:T(1024)(128)(4,1)S(1)} %not.7), kind=kLoop, calls=%fused_computation.1 | loop fusion | flops 6290432 | bytes 9216 | tf_op jit(solution)/shard_map/reduce_sum | solution.py:26
  8.1 0.7 %add_select_fusion = s32[1024]{0:T(1024)S(1)} fusion(pred[1024]{0:T(1024)(128)(4,1)S(1)} %fusion.5, s32[1024]{0:T(1024)S(1)} %convert_reduce_fusion, s32[1024]{0:T(1024)} %param.9), kind=kLoop, calls=%fused_computation.17 | loop fusion | flops 3072 | bytes 13312 | tf_op jit(solution)/shard_map/jit(_where)/select_n | solution.py:27
  8.8 0.1 reshape.14.fresh_ref
  8.9 0.9 %fusion.1.picks_ref = bf16[1024,1024]{1,0:T(8,128)(2,1)S(1)} fusion(s32[1024]{0:T(1024)S(1)} %add_select_fusion), kind=kLoop, calls=%fused_computation.4 | loop fusion | flops 2097152 | bytes 2101248 | tf_op jit(solution)/shard_map/convert_element_type | solution.py:28
  9.8 0.0 collective-permute-done.halo_ref
  9.8 0.0 copy-done.1
  9.8 0.0 copy-done.2
  9.8 0.0 copy-start
  9.9 2.2 %copy-done = bf16[1024,2048]{1,0:T(8,128)(2,1)S(1)} copy-done((bf16[1024,2048]{1,0:T(8,128)(2,1)S(1)}, bf16[1024,2048]{1,0:T(8,128)(2,1)}, u32[]{:S(2)}) %copy-start) | copy-done | bytes 4194328
  12.0 20.3 %shard_map.64 = bf16[8,4,32,256]{3,2,1,0:T(8,128)(2,1)S(1)} custom-call(bf16[11,8,1024]{2,1,0:T(8,128)(2,1)S(1)} %collective-permute-done.halo_ref, bf16[32,8,1024]{2,1,0:T(8,128)(2,1)S(1)} %reshape.14.fresh_ref, f32[12,1024]{1,0:T(8,128)S(1)} %copy-done.2, bf16[1024,2048]{1,0:T(8,128)(2,1)S(1)} %copy-done, bf16[1024,1024]{1,0:T(8,128)(2,1)S(1)} %fusion.1.picks_ref, ...), custom_call_target="tpu_custom_call" | custom-call | tf_op jit(solution)/shard_map/pallas_call | solution.py:150
  32.3 0.3 copy.22
  32.6 0.1 fusion.9
  32.7 0.1 maximum_bitcast_fusion
  32.8 1.5 %convolution_multiply_fusion = f32[32,2,32,32]{3,2,1,0:T(8,128)} fusion(bf16[32,1,32,256]{3,2,1,0:T(8,128)(2,1)S(1)} %maximum_bitcast_fusion, bf16[32,1,32,256]{3,2,1,0:T(8,128)(2,1)S(1)} %bitcast.21, bf16[32,32,256]{2,1,0:T(8,128)(2,1)S(1)} %bitcast.19), kind=kOutput, calls=%fused_computation.5 | convolution fusion | flops 34144256 | bytes 1835008 | tf_op jit(solution)/shard_map/cpit,cjt->cpij/dot_general | solution.py:216
  (1 shorter events, 0.0 us)
Async XLA Ops:
  0.0 9.8 %copy-start.1 = (bf16[1024,1024]{1,0:T(8,128)(2,1)S(1)}, bf16[1024,1024]{1,0:T(8,128)(2,1)}, u32[]{:S(2)}) copy-start(bf16[1024,1024]{1,0:T(8,128)(2,1)} %constant.16.clone.order_ref) | copy-start | bytes 6291460
  0.0 9.8 %copy-start.2 = (f32[12,1024]{1,0:T(8,128)S(1)}, f32[12,1024]{1,0:T(8,128)}, u32[]{:S(2)}) copy-start(f32[12,1024]{1,0:T(8,128)} %taps_ref.1) | copy-start | bytes 147460
  2.0 7.8 %collective-permute-start = (bf16[11,8,1024]{2,1,0:T(8,128)(2,1)}, bf16[11,8,1024]{2,1,0:T(8,128)(2,1)S(1)}, u32[]{:S(2)}, u32[]{:S(2)}) collective-permute-start(bf16[11,8,1024]{2,1,0:T(8,128)(2,1)} %slice.13), channel_id=1, source_target_pairs={{0,1},{1,2},{2,3},{4,5},{5,6},{6,7},{8,9},{9,10},{10,11},{12,13},{... | collective-permute-start | bytes 540680 | tf_op jit(solution)/shard_map/ppermute | solution.py:187
  9.8 2.2 %copy-start = (bf16[1024,2048]{1,0:T(8,128)(2,1)S(1)}, bf16[1024,2048]{1,0:T(8,128)(2,1)}, u32[]{:S(2)}) copy-start(bf16[1024,2048]{1,0:T(8,128)(2,1)} %constant.15.clone.table) | copy-start | bytes 12582916

commit v3 on v2

--- a/solution.py
+++ b/solution.py
@@ -32,12 +32,47 @@
 MESH = pl.DeviceIdType.MESH
 
 
-def turn_kernel(chans, times, halo_ref, fresh_ref, taps_ref, table, picks_ref, order_ref, out_ref, wide, both_ref, spectra, got_ref, sending, send_sem, recv_sem):
+def spread(row):
+    return jnp.concatenate(
+        [jnp.transpose(jnp.broadcast_to(row[:, i : i + 128], (128, 128))) for i in range(0, row.shape[1], 128)], axis=0
+    )
+
+
+def slot_row(flagged, owners, capacity):
+    channels = owners.shape[1]
+    owner = owners.astype(jnp.float32)
+    marks = spread(flagged.astype(jnp.float32))
+    ids = lax.broadcasted_iota(jnp.int32, (1, channels), 1).astype(jnp.float32)
+    dead = jnp.concatenate(
+        [
+            jnp.sum(jnp.where(marks == ids[:, i : i + 128], 1.0, 0.0), axis=0, keepdims=True)
+            for i in range(0, channels, 128)
+        ],
+        axis=1,
+    )
+    keys = spread(jnp.where(dead > 0.0, -1.0, owner))
+    ranks = []
+    for i in range(0, channels, 128):
+        ahead = keys[: i + 128]
+        at = lax.broadcasted_iota(jnp.int32, ahead.shape, 0)
+        here = lax.broadcasted_iota(jnp.int32, ahead.shape, 1) + i
+        same = (ahead == owner[:, i : i + 128]) & (at < here)
+        ranks.append(jnp.sum(jnp.where(same, 1.0, 0.0), axis=0, keepdims=True))
+    return jnp.where(dead > 0.0, -1.0, owner * capacity + jnp.concatenate(ranks, axis=1))
+
+
+def turn_kernel(chans, times, fresh_ref, taps_ref, flagged_ref, owners_ref, table_hbm, order_hbm, out_ref, table, order_ref, halo_ref, wide, both_ref, spectra, got_ref, sending, fetch_sem, halo_sem, send_sem, recv_sem):
     devices = chans * times
     capacity, rows_all = sending.shape[1:]
     channels = table.shape[0]
     stations = out_ref.shape[1]
-    halo, spec_dev = halo_ref.shape[0], fresh_ref.shape[0]
+    halo = taps_ref.shape[0] - 1
+    pairs, back = fresh_ref.shape[0], halo_ref.shape[0]
+    series = fresh_ref.shape[1] // 2
+    chan, time = lax.axis_index("chan"), lax.axis_index("tm")
+    fetch_table = pltpu.make_async_copy(table_hbm, table, fetch_sem.at[0])
+    fetch_order = pltpu.make_async_copy(order_hbm, order_ref, fetch_sem.at[1])
+    fetch_table.start()
     per_group = GROUP_ROWS // capacity
     groups = devices // per_group
     me = lax.axis_index("chan") * times + lax.axis_index("tm")
@@ -54,14 +89,45 @@
     def place(source):
         return lax.rem(source, times) * chans + source // times
 
-    def widen(step, carry):
-        wide[halo + step] = fresh_ref[step].astype(jnp.float32)
-        return carry
-
-    for step in range(halo):
-        wide[step] = halo_ref[step].astype(jnp.float32)
-    lax.fori_loop(0, spec_dev, widen, 0)
-    series = fresh_ref.shape[1]
+    def halo_copy(other):
+        return pltpu.make_async_remote_copy(
+            src_ref=fresh_ref.at[pairs - back :],
+            dst_ref=halo_ref,
+            send_sem=halo_sem.at[0],
+            recv_sem=halo_sem.at[1],
+            device_id=(chan, other),
+            device_id_type=MESH,
+        )
+
+    def widen(pair, where):
+        both_times = pair.astype(jnp.float32)
+        wide[where] = both_times[:series]
+        wide[where + 1] = both_times[series:]
+
+    def widen_fresh(step, carry):
+        widen(fresh_ref[step], 2 * (back + step))
+        return carry
+
+    lax.fori_loop(0, pairs, widen_fresh, 0)
+    pl.semaphore_wait(barrier, devices - 1)
+
+    @pl.when(time < times - 1)
+    def _():
+        halo_copy(time + 1).start()
+
+    fetch_order.start()
+    slots = slot_row(flagged_ref[...], owners_ref[...], capacity)
+
+    @pl.when(time > 0)
+    def _():
+        halo_copy(time).wait_recv()
+        for step in range(back):
+            widen(halo_ref[step], 2 * step)
+
+    @pl.when(time == 0)
+    def _():
+        wide[: 2 * back] = jnp.zeros((2 * back, series, channels), jnp.float32)
+
     real_row = lax.broadcasted_iota(jnp.int32, (series, channels), 0) < series // 2
 
     def filter_two(step, carry):
@@ -69,7 +135,7 @@
         for half in range(2):
             total = jnp.zeros((series, channels), jnp.float32)
             for tap in range(halo + 1):
-                total = total + taps_ref[pl.ds(tap, 1), :] * wide[2 * step + half + halo - tap]
+                total = total + taps_ref[pl.ds(tap, 1), :] * wide[2 * step + half + 2 * back - tap]
             swapped = pltpu.roll(total, series // 2, 0)
             sums.append(total)
             turns.append(jnp.where(real_row, swapped, -swapped))
@@ -78,7 +144,8 @@
         both_ref[rows, channels:] = jnp.concatenate(turns, axis=0).astype(jnp.bfloat16)
         return carry
 
-    lax.fori_loop(0, spec_dev // 2, filter_two, 0)
+    lax.fori_loop(0, pairs, filter_two, 0)
+    fetch_table.wait()
 
     def block_copy(slot_block, source, other):
         return pltpu.make_async_remote_copy(
@@ -98,12 +165,12 @@
         return carry
 
     lax.fori_loop(0, channels // GROUP_ROWS, transform, 0)
-    pl.semaphore_wait(barrier, devices - 1)
 
     def send_group(step, carry):
         group = lax.rem(me // per_group + groups // 2 + step, groups)
-        rows = pl.ds(pl.multiple_of(group * GROUP_ROWS, GROUP_ROWS), GROUP_ROWS)
-        chosen = jnp.dot(picks_ref[rows, :], spectra[...], preferred_element_type=jnp.float32)
+        held = lax.broadcasted_iota(jnp.int32, (GROUP_ROWS, channels), 0) + group * GROUP_ROWS
+        picks = jnp.where(held.astype(jnp.float32) == slots, 1.0, 0.0).astype(jnp.bfloat16)
+        chosen = jnp.dot(picks, spectra[...], preferred_element_type=jnp.float32)
         sending[pl.ds(group * per_group, per_group)] = chosen.astype(jnp.bfloat16).reshape(
             per_group, capacity, chosen.shape[1]
         )
@@ -132,6 +199,11 @@
 
     lax.fori_loop(1, devices, finish, 0)
 
+    @pl.when(time < times - 1)
+    def _():
+        halo_copy(time + 1).wait_send()
+
+    fetch_order.wait()
     for station in range(stations):
         total = jnp.zeros((chans * capacity, rows_all), jnp.float32)
         for block in range(times):
@@ -143,28 +215,35 @@
         out_ref[:, station] = total.astype(jnp.bfloat16).reshape(chans, capacity, rows_all)
 
 
-def turn(before, fresh, filter_taps, table, picks, order, chans, times, capacity):
+def turn(fresh, filter_taps, flagged, owners, table, order, chans, times, capacity):
     devices = chans * times
-    spec_dev, series, channels = fresh.shape
-    rows = spec_dev * series
+    pairs, width, channels = fresh.shape
+    series = width // 2
+    rows = pairs * width
+    back = filter_taps.shape[0] // 2
     return pl.pallas_call(
         functools.partial(turn_kernel, chans, times),
         out_shape=jax.ShapeDtypeStruct((chans, series // 2, capacity, rows), jnp.bfloat16),
-        in_specs=[pl.BlockSpec(memory_space=pltpu.VMEM)] * 6,
+        in_specs=[pl.BlockSpec(memory_space=pltpu.VMEM)] * 4 + [pl.BlockSpec(memory_space=pl.ANY)] * 2,
         out_specs=pl.BlockSpec(memory_space=pltpu.VMEM),
         scratch_shapes=[
-            pltpu.VMEM((before.shape[0] + spec_dev, series, channels), jnp.float32),
+            pltpu.VMEM(table.shape, jnp.bfloat16),
+            pltpu.VMEM(order.shape, jnp.bfloat16),
+            pltpu.VMEM((back, width, channels), jnp.bfloat16),
+            pltpu.VMEM((2 * (back + pairs), series, channels), jnp.float32),
             pltpu.VMEM((rows, 2 * channels), jnp.bfloat16),
             pltpu.VMEM((channels, rows), jnp.bfloat16),
             pltpu.VMEM((devices, capacity, rows), jnp.bfloat16),
             pltpu.VMEM((devices, capacity, rows), jnp.bfloat16),
+            pltpu.SemaphoreType.DMA((2,)),
+            pltpu.SemaphoreType.DMA((2,)),
             pltpu.SemaphoreType.DMA((devices,)),
             pltpu.SemaphoreType.DMA((devices,)),
         ],
         compiler_params=pltpu.CompilerParams(
-            collective_id=0, has_side_effects=True, vmem_limit_bytes=32 * 1024 * 1024
+            collective_id=0, has_side_effects=True, vmem_limit_bytes=57 * 1024 * 1024
         ),
-    )(before, fresh, filter_taps, table, picks, order)
+    )(fresh, filter_taps, flagged.reshape(1, -1), owners.reshape(1, -1), table, order)
 
 
 def lane_order(stations, spec_dev, blocks):
@@ -183,15 +262,18 @@
     capacity = channels // devices
     spectra_all = spec_dev * times
     rows = 2 * stations * spec_dev
-    fresh = voltages.transpose(1, 2, 0, 3).reshape(spec_dev, 2 * stations, channels)
-    before = lax.ppermute(fresh[spec_dev - halo :], "tm", [(i, i + 1) for i in range(times - 1)])
-    picks = slot_matrix(flagged, owners, channels, capacity)
+    fresh = voltages.transpose(1, 2, 0, 3)
     table = dft_table(channels)
     order = lane_order(stations, spec_dev, times)
-    if capacity % 16 == 0 and GROUP_ROWS % capacity == 0 and channels % GROUP_ROWS == 0:
-        first = turn(before, fresh, filter_taps, table, picks, order, chans, times, capacity)
+    even = halo % 2 == 1 and spec_dev % 2 == 0 and stations % 4 == 0
+    if even and capacity % 16 == 0 and GROUP_ROWS % capacity == 0 and channels % GROUP_ROWS == 0:
+        paired = fresh.reshape(spec_dev // 2, 4 * stations, channels)
+        first = turn(paired, filter_taps, flagged, owners, table, order, chans, times, capacity)
         first = first.reshape(chans * stations, capacity, 2 * spectra_all).transpose(1, 0, 2)
     else:
+        fresh = fresh.reshape(spec_dev, 2 * stations, channels)
+        before = lax.ppermute(fresh[spec_dev - halo :], "tm", [(i, i + 1) for i in range(times - 1)])
+        picks = slot_matrix(flagged, owners, channels, capacity)
         joined = jnp.concatenate([before, fresh]).astype(jnp.float32)
         running = jnp.zeros(fresh.shape, jnp.float32)
         for tap in range(halo + 1):

time: 34.7 us -> 33.4 us (0.963)
  Pallas kernels: 20.3 us -> 26.6 us
  other arithmetic: 3.99 us -> 0.14 us
  starting transfers between devices: 2.35 us -> 0 us
  local copies, waits for them, and re-layouts: 6.05 us -> 3.7 us
  matrix products: 1.53 us -> 2.67 us
    pallas_call x1, Pallas kernels: 20.3 us -> 26.6 us  [turn(): pl.pallas_call(functools.partial(turn_kernel, chans, times), out_shape=ja...]
    ppermute x1 -> x0, starting transfers between devices: 2.35 us -> none  [local(): lax.ppermute(fresh[spec_dev - halo:], 'tm', [(i, i + 1) for i in range(ti...]
    unnamed x6 -> x0, local copies, waits for them, and re-layouts: 2.19 us -> none
    slice x3 -> x0, local copies, waits for them, and re-layouts: 1.99 us -> none  [local(): fresh[spec_dev - halo:]]
    reduce_sum x1 -> x0, other arithmetic: 1.37 us -> none  [slot_matrix(): rank = jnp.sum(earlier.astype(jnp.int32), axis=1)]
    dot_general x1, matrix products: 1.53 us -> 2.67 us  [local(): jnp.einsum('cpit,cjt->cpij', stacked, first, preferred_element_type=jnp.f...]
    reshape x1, local copies, waits for them, and re-layouts: 0.29 us -> 1.33 us  [local(): first.reshape(chans * stations, capacity, 2 * spectra_all)]
    reduce_or x1 -> x0, other arithmetic: 0.89 us -> none  [slot_matrix(): alive = jnp.logical_not(jnp.any(flagged[:, None] == ids[None, :], axis=0))]
  transfers between devices with their start and end apart: 1 -> 0, of which waited for: 0 -> 0; matrix products, arithmetic and copies ran while one was open for 16% -> 0% of each run, Pallas kernels for 0% -> 0%
where the time goes in v3:
time: 33.4 us; the launch traced here: 33.1 us
  Pallas kernels  26.6 us (80%)
  local copies, waits for them, and re-layouts  3.7 us (11%)
  matrix products  2.67 us (8%)
    pallas_call x1, Pallas kernels, turn(): pl.pallas_call(functools.partial(turn_kernel, chans, times), out_shape=ja...  26.6 us
    dot_general x1, matrix products, local(): jnp.einsum('cpit,cjt->cpij', stacked, first, preferred_element_type=jnp.f...  2.67 us
    transpose x1, local copies, waits for them, and re-layouts, local(): fresh = voltages.transpose(1, 2, 0, 3)  1.45 us
    reshape x1, local copies, waits for them, and re-layouts, local(): first.reshape(chans * stations, capacity, 2 * spectra_all)  1.33 us
    reshape x1, local copies, waits for them, and re-layouts, local(): paired = fresh.reshape(spec_dev // 2, 4 * stations, channels)  0.92 us

profile of v3, /device:TPU:0, one launch (start us, length us, event | category | flops | bytes accessed | tf_op | source)
XLA Modules:
  0.0 33.1 jit_solution(3177925678699138407)
XLA Ops:
  0.0 1.4 %copy.7 = bf16[32,2,4,1024]{3,2,1,0:T(4,128)(2,1)S(1)} copy(bf16[32,2,4,1024]{3,1,0,2:T(2,128)(2,1)} %bitcast.24) | data formatting | bytes 1048576 | tf_op jit(solution)/shard_map/transpose | solution.py:265
  1.5 0.9 %reshape.12.fresh_ref = bf16[16,16,1024]{2,1,0:T(8,128)(2,1)} reshape(bf16[32,2,4,1024]{3,2,1,0:T(4,128)(2,1)S(1)} %copy.7) | data formatting | bytes 1048576 | tf_op jit(solution)/shard_map/reshape | solution.py:270
  2.4 26.6 %shard_map.64 = bf16[8,4,32,256]{3,2,1,0:T(8,128)(2,1)} custom-call(bf16[16,16,1024]{2,1,0:T(8,128)(2,1)} %reshape.12.fresh_ref, f32[12,1024]{1,0:T(8,128)} %taps_ref.1, s32[1,256]{1,0:T(1,128)} %bitcast.26, s32[1,1024]{1,0:T(1,128)} %bitcast.25, bf16[1024,2048]{1,0:T(8,128)(2,1)} %constant.7.clone.table_hbm, bf16[1024,1024]{1,0:T(8,128)(2,1)} %constant.8.clone.order_hbm), custom_call_target="tpu_custom_call" | custom-call | tf_op jit(solution)/shard_map/pallas_call | solution.py:224
  28.9 1.3 %copy.17 = bf16[32,32,256]{2,0,1:T(8,128)(2,1)S(1)} copy(bf16[32,32,256]{2,1,0:T(8,128)(2,1)} %bitcast.20) | data formatting | bytes 1048576 | tf_op jit(solution)/shard_map/reshape | solution.py:272
  30.3 0.1 fusion.6
  30.4 0.1 maximum_bitcast_fusion
  30.4 2.7 %convolution_multiply_fusion = f32[32,2,32,32]{3,2,1,0:T(8,128)} fusion(bf16[32,1,32,256]{3,2,1,0:T(8,128)(2,1)S(1)} %maximum_bitcast_fusion, bf16[32,1,32,256]{3,2,1,0:T(8,128)(2,1)S(1)} %bitcast.23, bf16[32,32,256]{2,1,0:T(8,128)(2,1)} %bitcast.21), kind=kOutput, calls=%fused_computation | convolution fusion | flops 34144256 | bytes 1835008 | tf_op jit(solution)/shard_map/cpit,cjt->cpij/dot_general | solution.py:298

commit v4 on v3

--- a/solution.py
+++ b/solution.py
@@ -241,7 +241,7 @@
             pltpu.SemaphoreType.DMA((devices,)),
         ],
         compiler_params=pltpu.CompilerParams(
-            collective_id=0, has_side_effects=True, vmem_limit_bytes=57 * 1024 * 1024
+            collective_id=0, has_side_effects=True, vmem_limit_bytes=52 * 1024 * 1024
         ),
     )(fresh, filter_taps, flagged.reshape(1, -1), owners.reshape(1, -1), table, order)
 

time: 33.4 us -> 30.7 us (0.919)
  Pallas kernels: 26.6 us -> 24.7 us
  matrix products: 2.67 us -> 1.52 us
  local copies, waits for them, and re-layouts: 3.7 us -> 4.06 us
    unnamed x0 -> x6, local copies, waits for them, and re-layouts: none -> 2.2 us
    pallas_call x1, Pallas kernels: 26.6 us -> 24.7 us  [turn(): pl.pallas_call(functools.partial(turn_kernel, chans, times), out_shape=ja...]
    dot_general x1, matrix products: 2.67 us -> 1.52 us  [local(): jnp.einsum('cpit,cjt->cpij', stacked, first, preferred_element_type=jnp.f...]
    reshape x1, local copies, waits for them, and re-layouts: 1.33 us -> 0.29 us  [local(): first.reshape(chans * stations, capacity, 2 * spectra_all)]
    reshape x1, local copies, waits for them, and re-layouts: 0.92 us -> 0.12 us  [local(): paired = fresh.reshape(spec_dev // 2, 4 * stations, channels)]
where the time goes in v4:
time: 30.7 us; the launch traced here: 30.5 us
  Pallas kernels  24.7 us (80%)
  local copies, waits for them, and re-layouts  4.06 us (13%)
  matrix products  1.52 us (5%)
    pallas_call x1, Pallas kernels, turn(): pl.pallas_call(functools.partial(turn_kernel, chans, times), out_shape=ja...  24.7 us
    unnamed x6, local copies, waits for them, and re-layouts  2.2 us
    dot_general x1, matrix products, local(): jnp.einsum('cpit,cjt->cpij', stacked, first, preferred_element_type=jnp.f...  1.52 us
    transpose x1, local copies, waits for them, and re-layouts, local(): fresh = voltages.transpose(1, 2, 0, 3)  1.45 us

profile of v4, /device:TPU:0, one launch (start us, length us, event | category | flops | bytes accessed | tf_op | source)
XLA Modules:
  0.0 30.5 jit_solution(17795960296248129529)
XLA Ops:
  0.0 1.4 %copy.7 = bf16[32,2,4,1024]{3,2,1,0:T(4,128)(2,1)S(1)} copy(bf16[32,2,4,1024]{3,1,0,2:T(2,128)(2,1)} %bitcast.26) | data formatting | bytes 1048576 | tf_op jit(solution)/shard_map/transpose | solution.py:265
  1.5 0.1 reshape.12.fresh_ref
  1.6 0.0 copy-start
  1.6 0.8 %copy-done = f32[12,1024]{1,0:T(8,128)S(1)} copy-done((f32[12,1024]{1,0:T(8,128)S(1)}, f32[12,1024]{1,0:T(8,128)}, u32[]{:S(2)}) %copy-start) | copy-done | bytes 49176
  2.4 0.0 copy-start.1
  2.4 0.7 %copy-done.1 = s32[1024]{0:T(1024)S(1)} copy-done((s32[1024]{0:T(1024)S(1)}, s32[1024]{0:T(1024)}, u32[]{:S(2)}) %copy-start.1) | copy-done | bytes 4120
  3.1 0.0 copy-start.2
  3.1 0.7 %copy-done.2 = s32[256]{0:T(256)S(1)} copy-done((s32[256]{0:T(256)S(1)}, s32[256]{0:T(256)}, u32[]{:S(2)}) %copy-start.2) | copy-done | bytes 1048
  3.8 24.7 %shard_map.64 = bf16[8,4,32,256]{3,2,1,0:T(8,128)(2,1)S(1)} custom-call(bf16[16,16,1024]{2,1,0:T(8,128)(2,1)S(1)} %reshape.12.fresh_ref, f32[12,1024]{1,0:T(8,128)S(1)} %copy-done, s32[1,256]{1,0:T(1,128)S(1)} %bitcast.23, s32[1,1024]{1,0:T(1,128)S(1)} %bitcast.22, bf16[1024,2048]{1,0:T(8,128)(2,1)} %constant.7.clone.table_hbm, ...), custom_call_target="tpu_custom_call" | custom-call | tf_op jit(solution)/shard_map/pallas_call | solution.py:224
  28.5 0.3 copy.17
  28.8 0.1 fusion.6
  28.9 0.1 maximum_bitcast_fusion
  28.9 1.5 %convolution_multiply_fusion = f32[32,2,32,32]{3,2,1,0:T(8,128)} fusion(bf16[32,1,32,256]{3,2,1,0:T(8,128)(2,1)S(1)} %maximum_bitcast_fusion, bf16[32,1,32,256]{3,2,1,0:T(8,128)(2,1)S(1)} %bitcast.25, bf16[32,32,256]{2,1,0:T(8,128)(2,1)S(1)} %bitcast.21), kind=kOutput, calls=%fused_computation | convolution fusion | flops 34144256 | bytes 1835008 | tf_op jit(solution)/shard_map/cpit,cjt->cpij/dot_general | solution.py:298
Async XLA Ops:
  1.6 0.8 %copy-start = (f32[12,1024]{1,0:T(8,128)S(1)}, f32[12,1024]{1,0:T(8,128)}, u32[]{:S(2)}) copy-start(f32[12,1024]{1,0:T(8,128)} %taps_ref.1) | copy-start | bytes 147460
  2.4 0.7 %copy-start.1 = (s32[1024]{0:T(1024)S(1)}, s32[1024]{0:T(1024)}, u32[]{:S(2)}) copy-start(s32[1024]{0:T(1024)} %param.9) | copy-start | bytes 12292
  3.1 0.7 %copy-start.2 = (s32[256]{0:T(256)S(1)}, s32[256]{0:T(256)}, u32[]{:S(2)}) copy-start(s32[256]{0:T(256)} %param.8) | copy-start | bytes 3076

commit v5 on v4

--- a/solution.py
+++ b/solution.py
@@ -40,8 +40,8 @@
 
 def slot_row(flagged, owners, capacity):
     channels = owners.shape[1]
-    owner = owners.astype(jnp.float32)
-    marks = spread(flagged.astype(jnp.float32))
+    owner = owners
+    marks = spread(flagged)
     ids = lax.broadcasted_iota(jnp.int32, (1, channels), 1).astype(jnp.float32)
     dead = jnp.concatenate(
         [
@@ -61,12 +61,13 @@
     return jnp.where(dead > 0.0, -1.0, owner * capacity + jnp.concatenate(ranks, axis=1))
 
 
-def turn_kernel(chans, times, fresh_ref, taps_ref, flagged_ref, owners_ref, table_hbm, order_hbm, out_ref, table, order_ref, halo_ref, wide, both_ref, spectra, got_ref, sending, fetch_sem, halo_sem, send_sem, recv_sem):
+def turn_kernel(chans, times, flags, fresh_ref, taps_ref, table_hbm, order_hbm, out_ref, table, order_ref, halo_ref, wide, both_ref, spectra, got_ref, sending, fetch_sem, halo_sem, send_sem, recv_sem):
     devices = chans * times
     capacity, rows_all = sending.shape[1:]
     channels = table.shape[0]
     stations = out_ref.shape[1]
-    halo = taps_ref.shape[0] - 1
+    taps = taps_ref.shape[0] - 2
+    halo = taps - 1
     pairs, back = fresh_ref.shape[0], halo_ref.shape[0]
     series = fresh_ref.shape[1] // 2
     chan, time = lax.axis_index("chan"), lax.axis_index("tm")
@@ -116,7 +117,7 @@
         halo_copy(time + 1).start()
 
     fetch_order.start()
-    slots = slot_row(flagged_ref[...], owners_ref[...], capacity)
+    slots = slot_row(taps_ref[taps + 1 : taps + 2, :flags], taps_ref[taps : taps + 1, :], capacity)
 
     @pl.when(time > 0)
     def _():
@@ -221,10 +222,12 @@
     series = width // 2
     rows = pairs * width
     back = filter_taps.shape[0] // 2
+    flags = jnp.pad(flagged, (0, channels - flagged.size))
+    small = jnp.concatenate([filter_taps, owners.astype(jnp.float32)[None], flags.astype(jnp.float32)[None]])
     return pl.pallas_call(
-        functools.partial(turn_kernel, chans, times),
+        functools.partial(turn_kernel, chans, times, flagged.size),
         out_shape=jax.ShapeDtypeStruct((chans, series // 2, capacity, rows), jnp.bfloat16),
-        in_specs=[pl.BlockSpec(memory_space=pltpu.VMEM)] * 4 + [pl.BlockSpec(memory_space=pl.ANY)] * 2,
+        in_specs=[pl.BlockSpec(memory_space=pltpu.VMEM)] * 2 + [pl.BlockSpec(memory_space=pl.ANY)] * 2,
         out_specs=pl.BlockSpec(memory_space=pltpu.VMEM),
         scratch_shapes=[
             pltpu.VMEM(table.shape, jnp.bfloat16),
@@ -243,7 +246,7 @@
         compiler_params=pltpu.CompilerParams(
             collective_id=0, has_side_effects=True, vmem_limit_bytes=52 * 1024 * 1024
         ),
-    )(fresh, filter_taps, flagged.reshape(1, -1), owners.reshape(1, -1), table, order)
+    )(fresh, small, table, order)
 
 
 def lane_order(stations, spec_dev, blocks):

time: 30.7 us -> 31.1 us (1.013)
  other arithmetic: 0.14 us -> 2.37 us
  local copies, waits for them, and re-layouts: 4.06 us -> 1.86 us
    unnamed x6 -> x0, local copies, waits for them, and re-layouts: 2.2 us -> none
    convert_element_type x0 -> x2, other arithmetic: none -> 1.37 us  [the longest x1 0.69 us: turn(): owners.astype(jnp.float32)[None]]
    concatenate x0 -> x1, other arithmetic: none -> 0.86 us  [turn(): jnp.concatenate([filter_taps, owners.astype(jnp.float32)[None], flags.ast...]
where the time goes in v5:
time: 31.1 us; the launch traced here: 30.8 us
  Pallas kernels  24.9 us (80%)
  other arithmetic  2.37 us (8%)
  local copies, waits for them, and re-layouts  1.86 us (6%)
  matrix products  1.62 us (5%)
    pallas_call x1, Pallas kernels, turn(): pl.pallas_call(functools.partial(turn_kernel, chans, times, flagged.size)...  24.9 us
    dot_general x1, matrix products, local(): jnp.einsum('cpit,cjt->cpij', stacked, first, preferred_element_type=jnp.f...  1.62 us
    transpose x1, local copies, waits for them, and re-layouts, local(): fresh = voltages.transpose(1, 2, 0, 3)  1.45 us
    concatenate x1, other arithmetic, turn(): jnp.concatenate([filter_taps, owners.astype(jnp.float32)[None], flags.ast...  0.86 us
    convert_element_type x1, other arithmetic, turn(): owners.astype(jnp.float32)[None]  0.69 us
    convert_element_type x1, other arithmetic, turn(): flags.astype(jnp.float32)[None]  0.68 us

profile of v5, /device:TPU:0, one launch (start us, length us, event | category | flops | bytes accessed | tf_op | source)
XLA Modules:
  0.0 30.8 jit_solution(13039576596558418194)
XLA Ops:
  0.0 0.7 %pad_convert_fusion = f32[1024]{0:T(1024)S(1)} fusion(s32[256]{0:T(256)} %param.8), kind=kLoop, calls=%fused_computation.11 | loop fusion | flops 1024 | bytes 5120 | tf_op jit(solution)/shard_map/convert_element_type | solution.py:226
  0.7 0.7 %convert_element_type.6 = f32[1024]{0:T(1024)S(1)} convert(s32[1024]{0:T(1024)} %param.9) | non-fusion elementwise | flops 1024 | bytes 8192 | tf_op jit(solution)/shard_map/convert_element_type | solution.py:226
  1.4 0.9 %pad_maximum_fusion.taps_ref = f32[14,1024]{1,0:T(8,128)S(1)} fusion(f32[1,1024]{1,0:T(1,128)S(1)} %bitcast.25, f32[1,1024]{1,0:T(1,128)S(1)} %bitcast.26, f32[12,1024]{1,0:T(8,128)} %param.7), kind=kLoop, calls=%fused_computation.10 | loop fusion | flops 28672 | bytes 114688 | tf_op jit(solution)/shard_map/concatenate | solution.py:226
  2.2 1.5 %copy.7 = bf16[32,2,4,1024]{3,2,1,0:T(4,128)(2,1)S(1)} copy(bf16[32,2,4,1024]{3,1,0,2:T(2,128)(2,1)} %bitcast.24) | data formatting | bytes 1048576 | tf_op jit(solution)/shard_map/transpose | solution.py:268
  3.7 0.1 reshape.6.fresh_ref
  3.8 24.9 %shard_map.64 = bf16[8,4,32,256]{3,2,1,0:T(8,128)(2,1)S(1)} custom-call(bf16[16,16,1024]{2,1,0:T(8,128)(2,1)S(1)} %reshape.6.fresh_ref, f32[14,1024]{1,0:T(8,128)S(1)} %pad_maximum_fusion.taps_ref, bf16[1024,2048]{1,0:T(8,128)(2,1)} %constant.9.clone.table_hbm, bf16[1024,1024]{1,0:T(8,128)(2,1)} %constant.10.clone.order_hbm), custom_call_target="tpu_custom_call" | custom-call | tf_op jit(solution)/shard_map/pallas_call | solution.py:227
  28.8 0.3 copy.17
  29.1 0.1 fusion.6
  29.1 0.1 maximum_bitcast_fusion
  29.2 1.6 %convolution_multiply_fusion = f32[32,2,32,32]{3,2,1,0:T(8,128)} fusion(bf16[32,1,32,256]{3,2,1,0:T(8,128)(2,1)S(1)} %maximum_bitcast_fusion, bf16[32,1,32,256]{3,2,1,0:T(8,128)(2,1)S(1)} %bitcast.23, bf16[32,32,256]{2,1,0:T(8,128)(2,1)S(1)} %bitcast.21), kind=kOutput, calls=%fused_computation | convolution fusion | flops 34144256 | bytes 1835008 | tf_op jit(solution)/shard_map/cpit,cjt->cpij/dot_general | solution.py:301

commit v6 on v4

--- a/solution.py
+++ b/solution.py
@@ -167,7 +167,7 @@
     lax.fori_loop(0, channels // GROUP_ROWS, transform, 0)
 
     def send_group(step, carry):
-        group = lax.rem(me // per_group + groups // 2 + step, groups)
+        group = lax.rem(me // per_group + groups - 1 - step, groups)
         held = lax.broadcasted_iota(jnp.int32, (GROUP_ROWS, channels), 0) + group * GROUP_ROWS
         picks = jnp.where(held.astype(jnp.float32) == slots, 1.0, 0.0).astype(jnp.bfloat16)
         chosen = jnp.dot(picks, spectra[...], preferred_element_type=jnp.float32)

time: 30.7 us -> 32.1 us (1.046)
  Pallas kernels: 24.7 us -> 26.1 us
    pallas_call x1, Pallas kernels: 24.7 us -> 26.1 us  [turn(): pl.pallas_call(functools.partial(turn_kernel, chans, times), out_shape=ja...]
where the time goes in v6:
time: 32.1 us; the launch traced here: 31.8 us
  Pallas kernels  26.1 us (81%)
  local copies, waits for them, and re-layouts  4.06 us (13%)
  matrix products  1.52 us (5%)
    pallas_call x1, Pallas kernels, turn(): pl.pallas_call(functools.partial(turn_kernel, chans, times), out_shape=ja...  26.1 us
    unnamed x6, local copies, waits for them, and re-layouts  2.2 us
    dot_general x1, matrix products, local(): jnp.einsum('cpit,cjt->cpij', stacked, first, preferred_element_type=jnp.f...  1.52 us
    transpose x1, local copies, waits for them, and re-layouts, local(): fresh = voltages.transpose(1, 2, 0, 3)  1.45 us

profile of v6, /device:TPU:0, one launch (start us, length us, event | category | flops | bytes accessed | tf_op | source)
XLA Modules:
  0.0 31.8 jit_solution(9528370641557082883)
XLA Ops:
  0.0 1.4 %copy.7 = bf16[32,2,4,1024]{3,2,1,0:T(4,128)(2,1)S(1)} copy(bf16[32,2,4,1024]{3,1,0,2:T(2,128)(2,1)} %bitcast.26) | data formatting | bytes 1048576 | tf_op jit(solution)/shard_map/transpose | solution.py:265
  1.5 0.1 reshape.12.fresh_ref
  1.6 0.0 copy-start
  1.6 0.8 %copy-done = f32[12,1024]{1,0:T(8,128)S(1)} copy-done((f32[12,1024]{1,0:T(8,128)S(1)}, f32[12,1024]{1,0:T(8,128)}, u32[]{:S(2)}) %copy-start) | copy-done | bytes 49176
  2.4 0.0 copy-start.1
  2.4 0.7 %copy-done.1 = s32[1024]{0:T(1024)S(1)} copy-done((s32[1024]{0:T(1024)S(1)}, s32[1024]{0:T(1024)}, u32[]{:S(2)}) %copy-start.1) | copy-done | bytes 4120
  3.1 0.0 copy-start.2
  3.1 0.7 %copy-done.2 = s32[256]{0:T(256)S(1)} copy-done((s32[256]{0:T(256)S(1)}, s32[256]{0:T(256)}, u32[]{:S(2)}) %copy-start.2) | copy-done | bytes 1048
  3.8 26.1 %shard_map.64 = bf16[8,4,32,256]{3,2,1,0:T(8,128)(2,1)S(1)} custom-call(bf16[16,16,1024]{2,1,0:T(8,128)(2,1)S(1)} %reshape.12.fresh_ref, f32[12,1024]{1,0:T(8,128)S(1)} %copy-done, s32[1,256]{1,0:T(1,128)S(1)} %bitcast.23, s32[1,1024]{1,0:T(1,128)S(1)} %bitcast.22, bf16[1024,2048]{1,0:T(8,128)(2,1)} %constant.7.clone.table_hbm, ...), custom_call_target="tpu_custom_call" | custom-call | tf_op jit(solution)/shard_map/pallas_call | solution.py:224
  29.9 0.3 copy.17
  30.2 0.1 fusion.6
  30.2 0.1 maximum_bitcast_fusion
  30.3 1.5 %convolution_multiply_fusion = f32[32,2,32,32]{3,2,1,0:T(8,128)} fusion(bf16[32,1,32,256]{3,2,1,0:T(8,128)(2,1)S(1)} %maximum_bitcast_fusion, bf16[32,1,32,256]{3,2,1,0:T(8,128)(2,1)S(1)} %bitcast.25, bf16[32,32,256]{2,1,0:T(8,128)(2,1)S(1)} %bitcast.21), kind=kOutput, calls=%fused_computation | convolution fusion | flops 34144256 | bytes 1835008 | tf_op jit(solution)/shard_map/cpit,cjt->cpij/dot_general | solution.py:298
Async XLA Ops:
  1.6 0.8 %copy-start = (f32[12,1024]{1,0:T(8,128)S(1)}, f32[12,1024]{1,0:T(8,128)}, u32[]{:S(2)}) copy-start(f32[12,1024]{1,0:T(8,128)} %taps_ref.1) | copy-start | bytes 147460
  2.4 0.7 %copy-start.1 = (s32[1024]{0:T(1024)S(1)}, s32[1024]{0:T(1024)}, u32[]{:S(2)}) copy-start(s32[1024]{0:T(1024)} %param.9) | copy-start | bytes 12292
  3.1 0.7 %copy-start.2 = (s32[256]{0:T(256)S(1)}, s32[256]{0:T(256)}, u32[]{:S(2)}) copy-start(s32[256]{0:T(256)} %param.8) | copy-start | bytes 3076
